TPU v7x, 256 devices: a whole 4x4x8 slice. The times are simulated.
256 devices in a mesh: len: 64 (over z, y, core), sec: 4 (over x).
Axes of the slice: x: 4, y: 4, z: 8, core: 2. Of those that a mesh axis runs over, the one named last changes fastest.
Arguments:
- predicted: float32 [3, 1024, 128, 128], P(None, 'len', 'sec'), may hold values from -6 to 6
- material: int32 [1024, 128, 128], P('len', 'sec'), may hold values from 0 to 7
- stiffness_table: float32 [8], replicated, may hold values from 1 to 10
- density_table: float32 [8], replicated, may hold values from 0.5 to 2
- contact_tile: int32 [4096, 1], P('len'), may hold values from 0 to 63; in each aligned block of 64 rows (0 to 63, 64 to 127, ...) at most 2 rows name the same one
- contact_row: int32 [4096], P('len'), may hold values from 0 to 2047
- contact_force: float32 [4096, 3, 128], P('len'), may hold values from -6 to 6
Outputs:
- displacement: float32 [3, 1024, 128, 128], P(None, 'len', 'sec')
- residual: float32 [3, 1024, 128, 128], P(None, 'len', 'sec')
Inputs may be any that keep to these rules, and one draw needn't show every extreme that they name: `contact_tile`: within the 64 rows of each index of len, no tile is named more than 2 times, a bound that some block reaches.
All inputs are finite; a program needn't handle non-finite values.
Results may differ from a plain program's by a relative error of at most 0.0003.
Values sent between devices are 32-bit elements; how exact they have to be, the bound alone decides.
A program may use at most 64 MiB of HBM per device.

v0:
```python
import jax
import jax.numpy as jnp
from jax import lax
from jax.experimental import pallas as pl
from jax.experimental.pallas import tpu as pltpu
from jax.sharding import PartitionSpec as P

MESH = pl.DeviceIdType.MESH
F32 = jnp.float32
BF16 = jnp.bfloat16
LEN, SEC = 64, 4
AROUND = [(0, 1), (0, -1), (1, 0), (-1, 0), (1, 1), (1, -1), (-1, 1), (-1, -1)]
XE, TF = 32, 6
X1, T1 = 16, 3
X2 = 8


def shift_depth(w):
    lane = lax.broadcasted_iota(jnp.int32, w.shape, w.ndim - 1)
    low = jnp.where(lane == 0, 0.0, pltpu.roll(w, 1, w.ndim - 1))
    high = jnp.where(lane == 127, 0.0, pltpu.roll(w, 127, w.ndim - 1))
    return low + high


def shift_rows(w):
    tiles = w.shape[0]
    below = jnp.concatenate([pltpu.roll(w[tiles - 1 :], 1, 1), w[: tiles - 1]], axis=0)
    above = jnp.concatenate([w[1:], pltpu.roll(w[:1], 7, 1)], axis=0)
    return below + above


def around(ref, c, x, scale):
    w = ref[c, x]
    along = ref[c, x - 1] + ref[c, x + 1]
    depth = shift_depth(w)
    if scale != 1.0:
        depth = scale * depth
    return w, 12.0 * along + (shift_rows(w) + depth)


def halves(value):
    high = value.astype(BF16)
    return high, (value - high.astype(F32)).astype(BF16)


def body(
    pred, mat, stiff, dens, tile, crow, force,
    out_v, out_r,
    pext, mext, sent, got, got_l, got_r,
    q0, m0, b0, ra0, e0, iq0,
    wa, wb, ff, aa,
    q1, m1, b1, ra1, e1, iq1,
    d1, a1, wc, wd, nat, deft,
    fac2, rq2, q2, iq2,
    slope_y, slope_z, g1, g2, z1, z2,
    s_first, r_first, s_ends, r_right, r_left,
    w1s, up_s, dn_s, up_r, dn_r,
    v2s, va_s, vb_s, va_r, vb_r, pn, on_v, on_r,
    sem_in, e_s, e_r, a_s, a_r, f_s, f_r, gs, gr, zs, zr, n_s, n_r, x_s, x_r, o_s,
):
    l = lax.axis_index("len")
    s = lax.axis_index("sec")
    z = l // 8
    r = lax.rem(l, 8)

    def there(dl, ds):
        return {
            "len": jnp.clip(l + dl, 0, LEN - 1),
            "sec": jnp.clip(s + ds, 0, SEC - 1),
        }

    def has(dl, ds):
        a, b = l + dl, s + ds
        return (a >= 0) & (a < LEN) & (b >= 0) & (b < SEC)

    def remote(src, dst, ssem, rsem, device):
        return pltpu.make_async_remote_copy(
            src_ref=src, dst_ref=dst, send_sem=ssem, recv_sem=rsem,
            device_id=device, device_id_type=MESH,
        )

    class Send:
        def __init__(self, src, dst, ssem, rsem, dl, ds):
            self.copy = remote(src, dst, ssem, rsem, there(dl, ds))
            self.to, self.back = has(dl, ds), has(-dl, -ds)

        def start(self):
            pl.when(self.to)(self.copy.start)

        def sent(self):
            pl.when(self.to)(self.copy.wait_send)

        def came(self):
            pl.when(self.back)(self.copy.wait_recv)

    late = []

    own_p = pltpu.make_async_copy(pred, pext.at[:, 8:24, 8:40, :], sem_in.at[0])
    own_m = pltpu.make_async_copy(mat, mext.at[8:24, 8:40, :], sem_in.at[1])
    own_p.start()
    own_m.start()

    def clear(ref, *at):
        shape = ref.at[at].shape if at else ref.shape
        ref[at if at else ...] = jnp.zeros(shape, ref.dtype)

    edge_l, edge_r, edge_d, edge_u = l == 0, l == LEN - 1, s == 0, s == SEC - 1
    every = slice(None)

    def clear_x(lo, hi):
        def step(x, _):
            for c in range(3):
                pext[c, x] = jnp.zeros((48, 128), F32)
            mext[x] = jnp.zeros((48, 128), jnp.int32)
            return 0

        lax.fori_loop(lo, hi, step, 0)

    def clear_rows(lo):
        def step(x, _):
            for c in range(3):
                pext[c, x, lo : lo + 8, :] = jnp.zeros((8, 128), F32)
            mext[x, lo : lo + 8, :] = jnp.zeros((8, 128), jnp.int32)
            return 0

        lax.fori_loop(0, XE, step, 0)

    @pl.when(edge_l)
    def _():
        clear_x(0, 8)
        clear(got_l)
        clear(r_left)

    @pl.when(edge_r)
    def _():
        clear_x(24, 32)
        clear(got_r)
        clear(r_first)
        clear(r_right)

    @pl.when(edge_d)
    def _():
        clear_rows(0)
        clear(up_r)
        clear(va_r)

    @pl.when(edge_u)
    def _():
        clear_rows(40)
        clear(dn_r)
        clear(vb_r)

    @pl.when(edge_l | edge_r | edge_d | edge_u)
    def _():
        def step(i, _):
            for k in range(2):
                for c in range(3):
                    nat[k, c, i] = jnp.zeros((24, 128), F32)
            return 0

        lax.fori_loop(0, X1, step, 0)

    barrier = pltpu.get_barrier_semaphore()

    def greet(k, _):
        pl.semaphore_signal(
            barrier, inc=1, device_id_type=MESH,
            device_id={"len": lax.rem(l + k, LEN), "sec": s},
        )
        return 0

    lax.fori_loop(1, LEN, greet, 0)
    met = LEN - 1
    for dl, ds in AROUND:
        if ds:
            met = met + jnp.where(has(dl, ds), 1, 0)

            @pl.when(has(dl, ds))
            def _(dl=dl, ds=ds):
                pl.semaphore_signal(barrier, inc=1, device_id_type=MESH, device_id=there(dl, ds))

    column = lax.broadcasted_iota(jnp.int32, (64, 64), 0)
    matches = (tile[...] == column).astype(F32)
    earlier = (column < lax.broadcasted_iota(jnp.int32, (64, 64), 1)).astype(BF16)
    before = jnp.dot(matches.astype(BF16), earlier, preferred_element_type=F32)
    picks = [matches * (before == k).astype(F32) for k in (0.0, 1.0)]
    keys = (crow[...] + 1).astype(F32)
    select = jnp.concatenate(picks, axis=0).astype(BF16)
    flat = jnp.concatenate([force[c] for c in range(3)], axis=1)
    packed = jnp.dot(
        jnp.concatenate([select, select], axis=1),
        jnp.concatenate(halves(flat), axis=0),
        preferred_element_type=F32,
    )
    for k in range(2):
        for c in range(3):
            sent[pl.ds(4 * k + c, 64, stride=8), :] = packed[64 * k : 64 * k + 64, 128 * c : 128 * c + 128]
        here = jnp.sum(picks[k] * keys, axis=1, keepdims=True)
        sent[pl.ds(4 * k + 3, 64, stride=8), :] = jnp.broadcast_to(here, (64, 128))

    def rows_of(t):
        return pl.ds(pl.multiple_of(t * 8, 8), 8)

    pl.semaphore_wait(barrier, met)

    def post(k, _):
        t = lax.rem(l + k, LEN)
        remote(sent.at[rows_of(t)], got.at[rows_of(l)], a_s.at[0], a_r.at[0], {"len": t, "sec": s}).start()
        return 0

    lax.fori_loop(1, LEN, post, 0)
    got[rows_of(l), :] = sent[rows_of(l), :]

    halo = []
    for i, (dl, ds) in enumerate(AROUND):
        sx = {1: slice(8, 16), -1: slice(0, 8), 0: slice(0, 16)}[dl]
        dx = {1: slice(0, 8), -1: slice(24, 32), 0: slice(8, 24)}[dl]
        sy = {1: slice(24, 32), -1: slice(0, 8), 0: slice(0, 32)}[ds]
        dy = {1: slice(0, 8), -1: slice(40, 48), 0: slice(8, 40)}[ds]
        halo.append(Send(mat.at[sx, sy, :], mext.at[dx, dy, :], e_s.at[2 * i], e_r.at[2 * i], dl, ds))
        halo.append(Send(pred.at[:, sx, sy, :], pext.at[:, dx, dy, :], e_s.at[2 * i + 1], e_r.at[2 * i + 1], dl, ds))
    for h in halo[::2] + halo[1::2]:
        h.start()
    late += halo
    own_m.wait()
    for h in halo[::2]:
        h.came()

    sub = lax.broadcasted_iota(jnp.int32, (8, 128), 0)

    def inside(x, y):
        return (x >= 0) & (x < 16 * LEN) & (y >= 0) & (y < 32 * SEC)

    def fine_coefficients(x, _):
        for j in range(TF):
            ids = mext[x, pl.ds(j, 8, stride=TF), :]
            stiffness = jnp.full((8, 128), stiff[0], F32)
            density = jnp.full((8, 128), dens[0], F32)
            for entry in range(1, 8):
                stiffness = jnp.where(ids == entry, stiff[entry], stiffness)
                density = jnp.where(ids == entry, dens[entry], density)
            grid = inside(l * 16 + x - 8, s * 32 - 8 + sub * TF + j)
            q = jnp.sqrt(stiffness)
            m = 0.05 * density
            d = m + 28.0 * stiffness
            iq = 1.0 / q
            rd = jnp.where(grid, 0.7 / d, 0.0)
            q0[x, j] = q
            m0[x, j] = m
            b0[x, j] = rd * stiffness
            ra0[x, j] = rd * q
            e0[x, j] = d * iq
            iq0[x, j] = iq
        return 0

    lax.fori_loop(0, XE, fine_coefficients, 0)

    def one_coefficients(x, _):
        for j in range(T1):
            q = 0.25 * ((q0[2 * x, 2 * j] + q0[2 * x + 1, 2 * j]) + (q0[2 * x, 2 * j + 1] + q0[2 * x + 1, 2 * j + 1]))
            m = 0.25 * ((m0[2 * x, 2 * j] + m0[2 * x + 1, 2 * j]) + (m0[2 * x, 2 * j + 1] + m0[2 * x + 1, 2 * j + 1]))
            grid = inside(l * 16 + 2 * x - 8, s * 32 - 8 + (sub * T1 + j) * 2)
            d = 4.0 * m + 34.0 * (q * q)
            iq = 1.0 / q
            rd = jnp.where(grid, 0.7 / d, 0.0)
            q1[x, j] = q
            m1[x, j] = m
            b1[x, j] = rd * (q * q)
            ra1[x, j] = rd * q
            e1[x, j] = d * iq
            iq1[x, j] = iq
        return 0

    lax.fori_loop(0, X1, one_coefficients, 0)

    def own_rows_of_pairs(slot, tiles):
        for j in range(T1):
            pn[slot, pl.ds(j, 8, stride=T1), :] = tiles[j]
        return pn[slot, pl.ds(4, 8, stride=2), :] + pn[slot, pl.ds(5, 8, stride=2), :]

    def two_coefficients(x, _):
        q = 0.25 * own_rows_of_pairs(0, [q1[2 * x, j] + q1[2 * x + 1, j] for j in range(T1)])
        m = 0.25 * own_rows_of_pairs(1, [m1[2 * x, j] + m1[2 * x + 1, j] for j in range(T1)])
        at = l * 4 + x - 2
        rd = jnp.where((at >= 0) & (at < 4 * LEN), 1.0, 0.0) / (16.0 * m + 58.0 * (q * q))
        q2[x] = q
        iq2[x] = 1.0 / q
        rq2[x] = rd * q
        fac2[x] = 56.0 * (rd * (q * q))
        return 0

    lax.fori_loop(0, X2, two_coefficients, 0)

    def gather_y(ref, value, i):
        ref[r] = value
        copies = []
        for k in range(1, 8):
            to = z * 8 + lax.rem(r + k, 8)
            copies.append(remote(ref.at[r], ref.at[r], gs.at[i, k], gr.at[i, k], {"len": to, "sec": s}))
        for copy in copies:
            copy.start()

        def came():
            for copy in copies:
                copy.wait_recv()

        def gone():
            for copy in copies:
                copy.wait_send()

        return came, gone

    def gather_z(ref, value, i):
        ref[z] = value
        copies = []
        for k in range(1, 8):
            to = lax.rem(z + k, 8) * 8 + r
            copies.append(remote(ref.at[z], ref.at[z], zs.at[i, k], zr.at[i, k], {"len": to, "sec": s}))
        for k, copy in enumerate(copies, 1):
            pl.when(z + k < 8)(copy.start)

        def came():
            for k, copy in enumerate(copies, 1):
                pl.when(z >= k)(copy.wait_recv)

        def gone():
            for k, copy in enumerate(copies, 1):
                pl.when(z + k < 8)(copy.wait_send)

        return came, gone

    came, gone_y0 = gather_y(slope_y, (fac2[2] * fac2[3]) * (fac2[4] * fac2[5]), 0)

    own_p.wait()
    for h in halo[1::2]:
        h.came()

    def start_fine(x, _):
        for j in range(TF):
            grid = inside(l * 16 + x - 8, s * 32 - 8 + sub * TF + j)
            for c in range(3):
                value = jnp.where(grid, pext[c, x, pl.ds(j, 8, stride=TF), :], 0.0)
                wa[c, x, j] = q0[x, j] * value
                ff[c, x, j] = m0[x, j] * value
        return 0

    lax.fori_loop(0, XE, start_fine, 0)

    came()
    ahead = lax.fori_loop(0, r, lambda k, p: p * slope_y[k], jnp.ones((8, 128), F32))
    whole = lax.fori_loop(r, 8, lambda k, p: p * slope_y[k], ahead)
    came, gone_z0 = gather_z(slope_z, whole, 0)

    every_row = remote(sent.at[0:504], got.at[0:504], a_s.at[0], a_r.at[0], there(0, 0))
    every_row.wait_recv()
    onward = [
        Send(got, got_l, f_s.at[0], f_r.at[0], 1, 0),
        Send(got, got_r, f_s.at[1], f_r.at[1], -1, 0),
    ]
    for h in onward:
        h.start()
    late += onward

    def add_loads(ref, block, first, x_local):
        lane = lax.broadcasted_iota(jnp.int32, (64, 128), 1)
        source = lax.broadcasted_iota(jnp.int32, (64, 128), 0)
        key = jnp.zeros((1, 128), F32)
        for k in range(2):
            rows = ref[pl.ds(4 * k + 3, 64, stride=8), :]
            key = key + jnp.sum(jnp.where(lane == source + 64 * k, rows, 0.0), axis=0, keepdims=True)
        flat = jnp.concatenate(
            [
                jnp.concatenate([ref[pl.ds(4 * k + c, 64, stride=8), :] for k in range(2)], axis=0)
                for c in range(3)
            ],
            axis=1,
        )
        values = jnp.concatenate(halves(flat), axis=0)
        shape = (4, TF, 8, 128)
        row = s * 32 - 8 + lax.broadcasted_iota(jnp.int32, shape, 2) * TF + lax.broadcasted_iota(jnp.int32, shape, 1)
        for part in range(2):
            cell = lax.broadcasted_iota(jnp.int32, shape, 0) + (x_local + 4 * part)
            cell = jnp.where((row >= 0) & (row < 32 * SEC), cell * 128 + row + 1, -1)
            hit = (cell.astype(F32) == key.reshape(1, 1, 1, 128)).astype(F32)
            hit = hit.reshape(4 * TF * 8, 128).astype(BF16)
            loads = jnp.dot(jnp.concatenate([hit, hit], axis=1), values, preferred_element_type=F32)
            at = first + 4 * part
            for c in range(3):
                total = ff[c, pl.ds(at, 4)] + loads[:, 128 * c : 128 * c + 128].reshape(shape)
                ff[c, pl.ds(at, 4)] = total
                aa[c, pl.ds(at, 4)] = ra0[pl.ds(at, 4)] * total

    add_loads(got, 0, 8, 0)
    add_loads(got, 1, 16, 8)
    onward[0].came()
    add_loads(got_l, 2, 0, 8)
    onward[1].came()
    add_loads(got_r, 3, 24, 0)

    def fine_sweep(src, dst, lo, hi):
        def step(x, _):
            for c in range(3):
                w, n = around(src, c, x, 1.0)
                dst[c, x] = (0.3 * w + aa[c, x]) + b0[x] * n
            return 0

        lax.fori_loop(lo, hi, step, 0)

    fine_sweep(wa, wb, 1, 31)
    fine_sweep(wb, wa, 2, 30)

    def defect_one(x, _):
        for c in range(3):
            total = None
            for i in range(2):
                at = 2 * x + i
                w, n = around(wa, c, at, 1.0)
                d = (ff[c, at] - e0[at] * w) + q0[at] * n
                total = d if total is None else total + d
            for j in range(T1):
                here = total[2 * j] + total[2 * j + 1]
                d1[c, x, j] = here
                a1[c, x, j] = ra1[x, j] * here
        return 0

    lax.fori_loop(2, 14, defect_one, 0)

    def first_correction(x, _):
        for c in range(3):
            w, n = around(a1, c, x, 4.0)
            wc[c, x] = 1.3 * w + b1[x] * n
        return 0

    lax.fori_loop(3, 13, first_correction, 0)

    def keep_own(x, _):
        for c in range(3):
            for k, ref in enumerate((a1, wc)):
                for j in range(T1):
                    pn[2 * c + k, pl.ds(j, 8, stride=T1), :] = ref[c, x, j]
                nat[k, c, x, 4:20, :] = pn[2 * c + k, 4:20, :]
        return 0

    for c in range(3):
        for x2 in range(4):
            total = None
            for i in range(2):
                x = 4 + 2 * x2 + i
                w, n = around(wc, c, x, 4.0)
                d = (d1[c, x] - e1[x] * w) + q1[x] * n
                total = d if total is None else total + d
            deft[c, x2] = own_rows_of_pairs(4 * c + x2, [total[j] for j in range(T1)])

    came()
    whole_z = jnp.ones((8, 128), F32)
    f = [fac2[x] for x in range(X2)]

    def chain(off):
        total = off[0]
        for x in range(1, 4):
            total = off[x] + f[2 + x] * total
        return total

    def carried_in(ref_y, came_y, ref_z, i):
        came_y()

        def join(k, total):
            return tuple(ref_y[k, c] + slope_y[k] * total[c] for c in range(3))

        zero = tuple(jnp.zeros((8, 128), F32) for _ in range(3))
        mine = lax.fori_loop(0, r, join, zero)
        whole = lax.fori_loop(r, 8, join, mine)
        came_z, gone_z = gather_z(ref_z, jnp.stack(whole), i)

        def finish():
            came_z()

            def join_z(k, total):
                return tuple(ref_z[k, c] + slope_z[k] * total[c] for c in range(3))

            before = lax.fori_loop(0, z, join_z, zero)
            return [mine[c] + ahead * before[c] for c in range(3)]

        return finish, gone_z

    off = [[rq2[2 + x] * deft[c, x] for x in range(4)] for c in range(3)]
    came, gone_y1 = gather_y(g1, jnp.stack([chain(off[c]) for c in range(3)]), 1)
    for c in range(3):
        s_first[c] = off[c][0]
    first = Send(s_first, r_first, n_s.at[0], n_r.at[0], -1, 0)
    first.start()
    late.append(first)

    lax.fori_loop(4, 12, keep_own, 0)
    nat_up = Send(nat.at[:, :, 4:12, 16:20, :], nat.at[:, :, 4:12, 0:4, :], x_s.at[0], x_r.at[0], 0, 1)
    nat_dn = Send(nat.at[:, :, 4:12, 4:8, :], nat.at[:, :, 4:12, 20:24, :], x_s.at[1], x_r.at[1], 0, -1)
    nat_up.start()
    nat_dn.start()
    late += [nat_up, nat_dn]

    finish, gone_z1 = carried_in(g1, came, z1, 1)
    nat_up.came()
    nat_dn.came()
    nat_right = Send(nat.at[:, :, 8:12], nat.at[:, :, 0:4], x_s.at[2], x_r.at[2], 1, 0)
    nat_left = Send(nat.at[:, :, 4:8], nat.at[:, :, 12:16], x_s.at[3], x_r.at[3], -1, 0)
    nat_right.start()
    nat_left.start()
    late += [nat_right, nat_left]
    first.came()
    carry = finish()

    w1 = []
    for c in range(3):
        line = []
        at = carry[c]
        for x in range(4):
            at = off[c][x] + f[2 + x] * at
            line.append(at)
        line.append(r_first[c] + f[6] * at)
        w1.append(line)
    for i in range(12):
        w1s[8 * i : 8 * i + 8, :] = w1[i // 4][i % 4]
    w1s[96:128, :] = jnp.zeros((32, 128), F32)
    up_s[...] = w1s[pl.ds(7, 16, stride=8), :]
    dn_s[...] = w1s[pl.ds(0, 16, stride=8), :]
    rows_up = Send(up_s, up_r, n_s.at[1], n_r.at[1], 0, 1)
    rows_dn = Send(dn_s, dn_r, n_s.at[2], n_r.at[2], 0, -1)
    rows_up.start()
    rows_dn.start()
    late += [rows_up, rows_dn]
    depth = [[16.0 * shift_depth(w1[c][x]) for x in range(4)] for c in range(3)]
    rows_up.came()
    rows_dn.came()
    off = []
    for c in range(3):
        line = []
        for x in range(4):
            i = 4 * c + x
            w = w1[c][x]
            below = jnp.where(sub == 0, up_r[i : i + 1, :], pltpu.roll(w, 1, 0))
            above = jnp.where(sub == 7, dn_r[i : i + 1, :], pltpu.roll(w, 7, 0))
            n = 12.0 * w1[c][x + 1] + ((below + above) + depth[c][x])
            line.append(rq2[2 + x] * (deft[c, x] + q2[2 + x] * n))
        off.append(line)

    came, gone_y2 = gather_y(g2, jnp.stack([chain(off[c]) for c in range(3)]), 2)
    for c in range(3):
        s_ends[c, 0] = off[c][0]
        s_ends[c, 1] = off[c][1]
        s_ends[c, 2] = off[c][3]
    to_left = Send(s_ends.at[:, 0:2], r_right, n_s.at[3], n_r.at[3], -1, 0)
    to_right = Send(s_ends.at[:, 2:3], r_left, n_s.at[4], n_r.at[4], 1, 0)
    to_left.start()
    to_right.start()
    late += [to_left, to_right]
    finish, gone_z2 = carried_in(g2, came, z2, 2)
    to_left.came()
    to_right.came()
    nat_right.came()
    nat_left.came()
    carry = finish()

    back = jnp.where(l > 0, 1.0, 0.0) / jnp.where(l > 0, f[1], 1.0)
    for c in range(3):
        line = [(carry[c] - r_left[c, 0]) * back, carry[c]]
        at = carry[c]
        for x in range(6):
            shift = off[c][x] if x < 4 else r_right[c, x - 4]
            at = shift + f[2 + x] * at
            line.append(at)
        for x in range(X2):
            i = 8 * (c * X2 + x)
            v2s[i : i + 8, :] = iq2[x] * line[x]
    for k in range(2):
        va_s[24 * k : 24 * k + 24, :] = v2s[pl.ds(6 + k, 24, stride=8), :]
        vb_s[24 * k : 24 * k + 24, :] = v2s[pl.ds(k, 24, stride=8), :]
    ends_up = Send(va_s, va_r, n_s.at[5], n_r.at[5], 0, 1)
    ends_dn = Send(vb_s, vb_r, n_s.at[6], n_r.at[6], 0, -1)
    ends_up.start()
    ends_dn.start()
    late += [ends_up, ends_dn]

    for i in range(24):
        v = v2s[8 * i : 8 * i + 8, :]
        pn[i, pl.ds(4, 8, stride=2), :] = v
        pn[i, pl.ds(5, 8, stride=2), :] = v
    ends_up.came()
    ends_dn.came()
    for i in range(24):
        for k in range(2):
            pn[i, 2 * k : 2 * k + 2, :] = jnp.broadcast_to(va_r[24 * k + i : 24 * k + i + 1, :], (2, 128))
            pn[i, 20 + 2 * k : 22 + 2 * k, :] = jnp.broadcast_to(vb_r[24 * k + i : 24 * k + i + 1, :], (2, 128))

    def correct_one(x2, _):
        for c in range(3):
            for j in range(T1):
                v = pn[c * X2 + x2, pl.ds(j, 8, stride=T1), :]
                for i in range(2):
                    x = 2 * x2 + i
                    a1[c, x, j] = nat[0, c, x, pl.ds(j, 8, stride=T1), :]
                    wc[c, x, j] = nat[1, c, x, pl.ds(j, 8, stride=T1), :] + q1[x, j] * v
        return 0

    lax.fori_loop(0, X2, correct_one, 0)

    def one_sweep(src, dst, lo, hi):
        def step(x, _):
            for c in range(3):
                w, n = around(src, c, x, 4.0)
                dst[c, x] = (0.3 * w + a1[c, x]) + b1[x] * n
            return 0

        lax.fori_loop(lo, hi, step, 0)

    one_sweep(wc, wd, 1, 15)
    one_sweep(wd, wc, 2, 14)

    def correct_fine(x, _):
        for c in range(3):
            v = iq1[x] * wc[c, x]
            for i in range(2):
                for j in range(TF):
                    at = 2 * x + i
                    wb[c, at, j] = wa[c, at, j] + q0[at, j] * v[j // 2]
        return 0

    lax.fori_loop(2, 14, correct_fine, 0)
    fine_sweep(wb, wa, 5, 27)
    fine_sweep(wa, wb, 6, 26)

    def results(x, _):
        for c in range(3):
            w, n = around(wb, c, x, 1.0)
            value = iq0[x] * w
            rest = (ff[c, x] - e0[x] * w) + q0[x] * n
            for j in range(TF):
                on_v[c, x - 8, pl.ds(j, 8, stride=TF), :] = value[j]
                on_r[c, x - 8, pl.ds(j, 8, stride=TF), :] = rest[j]
        return 0

    lax.fori_loop(8, 24, results, 0)
    outs = [
        pltpu.make_async_copy(on_v.at[:, :, 8:40, :], out_v, o_s.at[0]),
        pltpu.make_async_copy(on_r.at[:, :, 8:40, :], out_r, o_s.at[1]),
    ]
    for copy in outs:
        copy.start()
    every_row.wait_send()
    for h in late:
        h.sent()
    for gone in (gone_y0, gone_z0, gone_y1, gone_z1, gone_y2, gone_z2):
        gone()
    for copy in outs:
        copy.wait()


def shards(predicted, material, stiffness, density, tile, row, force):
    anywhere = pl.BlockSpec(memory_space=pl.ANY)
    vmem = pl.BlockSpec(memory_space=pltpu.VMEM)
    smem = pl.BlockSpec(memory_space=pltpu.SMEM)

    def v(*shape, dtype=F32):
        return pltpu.VMEM(shape, dtype)

    dma = pltpu.SemaphoreType.DMA
    scratch = [
        v(3, XE, 48, 128), v(XE, 48, 128, dtype=jnp.int32),
        v(512, 128), v(512, 128), v(512, 128), v(512, 128),
        *[v(XE, TF, 8, 128) for _ in range(6)],
        *[v(3, XE, TF, 8, 128) for _ in range(4)],
        *[v(X1, T1, 8, 128) for _ in range(6)],
        *[v(3, X1, T1, 8, 128) for _ in range(4)],
        v(2, 3, X1, 24, 128), v(3, 4, 8, 128),
        *[v(X2, 8, 128) for _ in range(4)],
        v(8, 8, 128), v(8, 8, 128),
        *[v(8, 3, 8, 128) for _ in range(4)],
        v(3, 8, 128), v(3, 8, 128), v(3, 3, 8, 128), v(3, 2, 8, 128), v(3, 1, 8, 128),
        v(128, 128), *[v(16, 128) for _ in range(4)],
        v(192, 128), *[v(48, 128) for _ in range(4)],
        v(24, 24, 128), v(3, 16, 48, 128), v(3, 16, 48, 128),
        dma((2,)), dma((16,)), dma((16,)), dma((1,)), dma((1,)), dma((2,)), dma((2,)),
        dma((3, 8)), dma((3, 8)), dma((3, 8)), dma((3, 8)),
        dma((7,)), dma((7,)), dma((4,)), dma((4,)), dma((2,)),
    ]
    result = jax.ShapeDtypeStruct(predicted.shape, F32)
    return pl.pallas_call(
        body,
        out_shape=(result, result),
        in_specs=[anywhere, anywhere, smem, smem, vmem, vmem, vmem],
        out_specs=(anywhere, anywhere),
        scratch_shapes=scratch,
        compiler_params=pltpu.CompilerParams(
            collective_id=0, has_side_effects=True, vmem_limit_bytes=48 * 2**20
        ),
    )(
        predicted, material, stiffness, density,
        tile.reshape(1, -1), row.reshape(1, -1), jnp.transpose(force, (1, 0, 2)),
    )


def solution(mesh):
    placed = (
        P(None, "len", "sec", None),
        P("len", "sec", None),
        P(),
        P(),
        P("len", None),
        P("len"),
        P("len", None, None),
    )
    return jax.shard_map(
        shards,
        mesh=mesh,
        in_specs=placed,
        out_specs=(P(None, "len", "sec", None), P(None, "len", "sec", None)),
        check_vma=False,
    )
```

profile of v0, /device:TPU:224, one launch (start us, length us, event | category | flops | bytes accessed | tf_op | source)
XLA Modules:
  0.0 82.0 jit_solution(13222430716535978633)
XLA Ops:
  0.6 0.0 copy-start.6
  0.6 0.0 copy-start.3
  0.7 0.0 copy-start.4
  0.7 0.0 copy-start.5
  0.7 0.6 copy-done.6
  1.3 0.0 copy-done.3
  1.3 0.0 copy-done.4
  1.3 0.0 copy-done.5
  1.3 0.0 copy-start
  1.3 1.1 %copy-done = f32[3,16,32,128]{3,2,1,0:T(8,128)S(1)} copy-done((f32[3,16,32,128]{3,2,1,0:T(8,128)S(1)}, f32[3,16,32,128]{3,2,1,0:T(8,128)}, u32[]{:S(2)}) %copy-start) | copy-done | bytes 786456
  2.5 0.0 copy-start.1
  2.5 0.9 %copy-done.1 = s32[16,32,128]{2,1,0:T(8,128)S(1)} copy-done((s32[16,32,128]{2,1,0:T(8,128)S(1)}, s32[16,32,128]{2,1,0:T(8,128)}, u32[]{:S(2)}) %copy-start.1) | copy-done | bytes 262168
  3.4 0.0 copy-start.2
  3.4 0.9 %copy-done.2 = f32[64,3,128]{2,0,1:T(8,128)S(1)} copy-done((f32[64,3,128]{2,0,1:T(8,128)S(1)}, f32[64,3,128]{2,0,1:T(8,128)}, u32[]{:S(2)}) %copy-start.2) | copy-done | bytes 98328
  4.3 76.0 %shard_map.86 = (f32[3,16,32,128]{3,2,1,0:T(8,128)S(1)}, f32[3,16,32,128]{3,2,1,0:T(8,128)S(1)}) custom-call(f32[3,16,32,128]{3,2,1,0:T(8,128)S(1)} %copy-done, s32[16,32,128]{2,1,0:T(8,128)S(1)} %copy-done.1, f32[8]{0:T(128)S(1)} %copy-done.3, f32[8]{0:T(128)S(1)} %copy-done.4, s32[1,64]{1,0:T(1,128)S(1)} %bitcast.4, s32[1,64]{1,0:T(1,128)S(1)} %bitcast.5, ...), custom_call_target="tpu_custom_call" | custom-call | tf_op jit(solution)/shard_map/pallas_call | solution.py:686
  80.3 0.9 %copy.11 = f32[3,16,32,128]{3,2,1,0:T(8,128)} copy(f32[3,16,32,128]{3,2,1,0:T(8,128)S(1)} %get-tuple-element.4) | data formatting | bytes 1572864
  81.2 0.9 %copy.12 = f32[3,16,32,128]{3,2,1,0:T(8,128)} copy(f32[3,16,32,128]{3,2,1,0:T(8,128)S(1)} %get-tuple-element.5) | data formatting | bytes 1572864
Async XLA Ops:
  0.6 0.7 copy-start.6
  0.6 0.7 copy-start.3
  0.7 0.7 copy-start.4
  0.7 0.7 copy-start.5
  1.3 1.1 %copy-start = (f32[3,16,32,128]{3,2,1,0:T(8,128)S(1)}, f32[3,16,32,128]{3,2,1,0:T(8,128)}, u32[]{:S(2)}) copy-start(f32[3,16,32,128]{3,2,1,0:T(8,128)} %pred_.1) | copy-start | bytes 2359300
  2.5 0.9 %copy-start.1 = (s32[16,32,128]{2,1,0:T(8,128)S(1)}, s32[16,32,128]{2,1,0:T(8,128)}, u32[]{:S(2)}) copy-start(s32[16,32,128]{2,1,0:T(8,128)} %mat.1) | copy-start | bytes 786436
  3.4 0.9 %copy-start.2 = (f32[64,3,128]{2,0,1:T(8,128)S(1)}, f32[64,3,128]{2,0,1:T(8,128)}, u32[]{:S(2)}) copy-start(f32[64,3,128]{2,0,1:T(8,128)} %param.13) | copy-start | bytes 294916
where the time goes:
time: 82.2 us; the launch traced here: 82 us
  Pallas kernels  76 us (92%)
  local copies, waits for them, and re-layouts  5.41 us (7%)
    pallas_call x1, Pallas kernels, shards(): pl.pallas_call(body, out_shape=(result, result), in_specs=[anywhere, anyw...  76 us
    unnamed x16, local copies, waits for them, and re-layouts  5.41 us

commit v1 on v0

--- a/solution.py
+++ b/solution.py
@@ -9,7 +9,8 @@
 F32 = jnp.float32
 BF16 = jnp.bfloat16
 LEN, SEC = 64, 4
-AROUND = [(0, 1), (0, -1), (1, 0), (-1, 0), (1, 1), (1, -1), (-1, 1), (-1, -1)]
+FINE_GROUP, ONE_GROUP = 4, 7
+FAR_FIRST = [4, 3, 5, 2, 6, 1, 7, 0]
 XE, TF = 32, 6
 X1, T1 = 16, 3
 X2 = 8
@@ -23,19 +24,34 @@
 
 
 def shift_rows(w):
-    tiles = w.shape[0]
-    below = jnp.concatenate([pltpu.roll(w[tiles - 1 :], 1, 1), w[: tiles - 1]], axis=0)
-    above = jnp.concatenate([w[1:], pltpu.roll(w[:1], 7, 1)], axis=0)
+    last = w.shape[1] - 1
+    below = jnp.concatenate([pltpu.roll(w[:, last:], 1, 2), w[:, :last]], axis=1)
+    above = jnp.concatenate([w[:, 1:], pltpu.roll(w[:, :1], 7, 2)], axis=1)
     return below + above
 
 
-def around(ref, c, x, scale):
-    w = ref[c, x]
-    along = ref[c, x - 1] + ref[c, x + 1]
+def around(ref, c, x, count, scale):
+    block = ref[c, pl.ds(x - 1, count + 2)]
+    w = block[1:-1]
     depth = shift_depth(w)
     if scale != 1.0:
         depth = scale * depth
-    return w, 12.0 * along + (shift_rows(w) + depth)
+    return w, 12.0 * (block[:-2] + block[2:]) + (shift_rows(w) + depth)
+
+
+def over(lo, hi, group, step):
+    rest = (hi - lo) % group
+    if rest:
+        step(lo, rest)
+    if hi - lo - rest == group:
+        step(lo + rest, group)
+    elif hi - lo > rest:
+
+        def turn(i, _):
+            step(lo + rest + i * group, group)
+            return 0
+
+        lax.fori_loop(0, (hi - lo) // group, turn, 0)
 
 
 def halves(value):
@@ -100,57 +116,61 @@
     own_p.start()
     own_m.start()
 
-    def clear(ref, *at):
-        shape = ref.at[at].shape if at else ref.shape
-        ref[at if at else ...] = jnp.zeros(shape, ref.dtype)
-
-    edge_l, edge_r, edge_d, edge_u = l == 0, l == LEN - 1, s == 0, s == SEC - 1
-    every = slice(None)
-
-    def clear_x(lo, hi):
-        def step(x, _):
+    def clear(ref):
+        ref[...] = jnp.zeros(ref.shape, ref.dtype)
+
+    barrier = pltpu.get_barrier_semaphore()
+
+    def greet_at(where):
+        pl.semaphore_signal(barrier, inc=1, device_id=where, device_id_type=MESH)
+
+    def greet(k, _):
+        greet_at({"len": lax.rem(l + k, LEN), "sec": s})
+        return 0
+
+    lax.fori_loop(2, LEN - 1, greet, 0)
+
+    def clear_x(x, _):
+        for c in range(3):
+            for side in (0, 24):
+                pext[c, side + x] = jnp.zeros((48, 128), F32)
+        for side in (0, 24):
+            mext[side + x] = jnp.zeros((48, 128), jnp.int32)
+        return 0
+
+    lax.fori_loop(0, 8, clear_x, 0)
+
+    def clear_rows(x, _):
+        for side in (0, 40):
             for c in range(3):
-                pext[c, x] = jnp.zeros((48, 128), F32)
-            mext[x] = jnp.zeros((48, 128), jnp.int32)
-            return 0
-
-        lax.fori_loop(lo, hi, step, 0)
-
-    def clear_rows(lo):
-        def step(x, _):
-            for c in range(3):
-                pext[c, x, lo : lo + 8, :] = jnp.zeros((8, 128), F32)
-            mext[x, lo : lo + 8, :] = jnp.zeros((8, 128), jnp.int32)
-            return 0
-
-        lax.fori_loop(0, XE, step, 0)
-
-    @pl.when(edge_l)
+                pext[c, x, side : side + 8, :] = jnp.zeros((8, 128), F32)
+            mext[x, side : side + 8, :] = jnp.zeros((8, 128), jnp.int32)
+        return 0
+
+    lax.fori_loop(8, 24, clear_rows, 0)
+
+    @pl.when(l == 0)
     def _():
-        clear_x(0, 8)
         clear(got_l)
         clear(r_left)
 
-    @pl.when(edge_r)
+    @pl.when(l == LEN - 1)
     def _():
-        clear_x(24, 32)
         clear(got_r)
         clear(r_first)
         clear(r_right)
 
-    @pl.when(edge_d)
+    @pl.when(s == 0)
     def _():
-        clear_rows(0)
         clear(up_r)
         clear(va_r)
 
-    @pl.when(edge_u)
+    @pl.when(s == SEC - 1)
     def _():
-        clear_rows(40)
         clear(dn_r)
         clear(vb_r)
 
-    @pl.when(edge_l | edge_r | edge_d | edge_u)
+    @pl.when((l == 0) | (l == LEN - 1) | (s == 0) | (s == SEC - 1))
     def _():
         def step(i, _):
             for k in range(2):
@@ -160,24 +180,12 @@
 
         lax.fori_loop(0, X1, step, 0)
 
-    barrier = pltpu.get_barrier_semaphore()
-
-    def greet(k, _):
-        pl.semaphore_signal(
-            barrier, inc=1, device_id_type=MESH,
-            device_id={"len": lax.rem(l + k, LEN), "sec": s},
-        )
-        return 0
-
-    lax.fori_loop(1, LEN, greet, 0)
+    for k in (1, LEN - 1):
+        greet(k, 0)
     met = LEN - 1
-    for dl, ds in AROUND:
-        if ds:
-            met = met + jnp.where(has(dl, ds), 1, 0)
-
-            @pl.when(has(dl, ds))
-            def _(dl=dl, ds=ds):
-                pl.semaphore_signal(barrier, inc=1, device_id_type=MESH, device_id=there(dl, ds))
+    for ds in (1, -1):
+        met = met + jnp.where(has(0, ds), 1, 0)
+        pl.when(has(0, ds))(lambda ds=ds: greet_at(there(0, ds)))
 
     column = lax.broadcasted_iota(jnp.int32, (64, 64), 0)
     matches = (tile[...] == column).astype(F32)
@@ -203,28 +211,61 @@
 
     pl.semaphore_wait(barrier, met)
 
-    def post(k, _):
-        t = lax.rem(l + k, LEN)
-        remote(sent.at[rows_of(t)], got.at[rows_of(l)], a_s.at[0], a_r.at[0], {"len": t, "sec": s}).start()
-        return 0
-
-    lax.fori_loop(1, LEN, post, 0)
+    def plane(g):
+        return lax.rem(z + g, 8)
+
+    for g in FAR_FIRST:
+
+        def post(i, _, g=g):
+            t = plane(g) * 8 + lax.rem(r + i, 8)
+            remote(sent.at[rows_of(t)], got.at[rows_of(l)], a_s.at[0], a_r.at[g], {"len": t, "sec": s}).start()
+            return 0
+
+        lax.fori_loop(0 if g else 1, 8, post, 0)
     got[rows_of(l), :] = sent[rows_of(l), :]
 
-    halo = []
-    for i, (dl, ds) in enumerate(AROUND):
-        sx = {1: slice(8, 16), -1: slice(0, 8), 0: slice(0, 16)}[dl]
-        dx = {1: slice(0, 8), -1: slice(24, 32), 0: slice(8, 24)}[dl]
-        sy = {1: slice(24, 32), -1: slice(0, 8), 0: slice(0, 32)}[ds]
-        dy = {1: slice(0, 8), -1: slice(40, 48), 0: slice(8, 40)}[ds]
-        halo.append(Send(mat.at[sx, sy, :], mext.at[dx, dy, :], e_s.at[2 * i], e_r.at[2 * i], dl, ds))
-        halo.append(Send(pred.at[:, sx, sy, :], pext.at[:, dx, dy, :], e_s.at[2 * i + 1], e_r.at[2 * i + 1], dl, ds))
-    for h in halo[::2] + halo[1::2]:
-        h.start()
-    late += halo
+    def halo(number, source, target, dl, ds):
+        return Send(source, target, e_s.at[number], e_r.at[number], dl, ds)
+
+    mat_sec = [
+        halo(0, mat.at[:, 24:32, :], mext.at[8:24, 0:8, :], 0, 1),
+        halo(1, mat.at[:, 0:8, :], mext.at[8:24, 40:48, :], 0, -1),
+    ]
+    pred_sec = [
+        halo(2, pred.at[:, :, 25:32, :], pext.at[:, 8:24, 1:8, :], 0, 1),
+        halo(3, pred.at[:, :, 0:7, :], pext.at[:, 8:24, 40:47, :], 0, -1),
+    ]
+    mat_len = [
+        halo(4, mat.at[8:16], mext.at[0:8, 8:40, :], 1, 0),
+        halo(5, mat.at[0:8], mext.at[24:32, 8:40, :], -1, 0),
+    ]
+    pred_len = [
+        halo(6, pred.at[:, 9:16], pext.at[:, 1:8, 8:40, :], 1, 0),
+        halo(7, pred.at[:, 0:7], pext.at[:, 24:31, 8:40, :], -1, 0),
+    ]
+    mat_corners, pred_corners = [], []
+    for i, (mrows, prows) in enumerate([(slice(0, 8), slice(2, 8)), (slice(40, 48), slice(40, 46))]):
+        mat_corners.append(halo(8 + i, mext.at[18:24, mrows, :], mext.at[2:8, mrows, :], 1, 0))
+        mat_corners.append(halo(10 + i, mext.at[8:14, mrows, :], mext.at[24:30, mrows, :], -1, 0))
+        pred_corners.append(halo(12 + i, pext.at[:, 18:24, prows, :], pext.at[:, 2:8, prows, :], 1, 0))
+        pred_corners.append(halo(14 + i, pext.at[:, 8:14, prows, :], pext.at[:, 24:30, prows, :], -1, 0))
+
+    def start(copies):
+        for copy in copies:
+            copy.start()
+        late.extend(copies)
+
+    def arrive(copies):
+        for copy in copies:
+            copy.came()
+
+    start(mat_sec)
+    start(pred_sec)
+    start(mat_len)
+    start(pred_len)
     own_m.wait()
-    for h in halo[::2]:
-        h.came()
+    arrive(mat_sec)
+    start(mat_corners)
 
     sub = lax.broadcasted_iota(jnp.int32, (8, 128), 0)
 
@@ -253,7 +294,7 @@
             iq0[x, j] = iq
         return 0
 
-    lax.fori_loop(0, XE, fine_coefficients, 0)
+    lax.fori_loop(8, 24, fine_coefficients, 0)
 
     def one_coefficients(x, _):
         for j in range(T1):
@@ -271,7 +312,7 @@
             iq1[x, j] = iq
         return 0
 
-    lax.fori_loop(0, X1, one_coefficients, 0)
+    lax.fori_loop(4, 12, one_coefficients, 0)
 
     def own_rows_of_pairs(slot, tiles):
         for j in range(T1):
@@ -289,7 +330,7 @@
         fac2[x] = 56.0 * (rd * (q * q))
         return 0
 
-    lax.fori_loop(0, X2, two_coefficients, 0)
+    lax.fori_loop(2, 6, two_coefficients, 0)
 
     def gather_y(ref, value, i):
         ref[r] = value
@@ -332,8 +373,8 @@
     came, gone_y0 = gather_y(slope_y, (fac2[2] * fac2[3]) * (fac2[4] * fac2[5]), 0)
 
     own_p.wait()
-    for h in halo[1::2]:
-        h.came()
+    arrive(pred_sec)
+    start(pred_corners)
 
     def start_fine(x, _):
         for j in range(TF):
@@ -341,27 +382,42 @@
             for c in range(3):
                 value = jnp.where(grid, pext[c, x, pl.ds(j, 8, stride=TF), :], 0.0)
                 wa[c, x, j] = q0[x, j] * value
-                ff[c, x, j] = m0[x, j] * value
-        return 0
-
-    lax.fori_loop(0, XE, start_fine, 0)
+                value = m0[x, j] * value
+                ff[c, x, j] = value
+                aa[c, x, j] = ra0[x, j] * value
+        return 0
+
+    lax.fori_loop(8, 24, start_fine, 0)
+
+    def fine_sweep(src, dst, lo, hi):
+        def step(x, count):
+            at = pl.ds(x, count)
+            for c in range(3):
+                w, n = around(src, c, x, count, 1.0)
+                dst[c, at] = (0.3 * w + aa[c, at]) + b0[at] * n
+
+        over(lo, hi, FINE_GROUP, step)
+
+    fine_sweep(wa, wb, 9, 23)
 
     came()
     ahead = lax.fori_loop(0, r, lambda k, p: p * slope_y[k], jnp.ones((8, 128), F32))
     whole = lax.fori_loop(r, 8, lambda k, p: p * slope_y[k], ahead)
     came, gone_z0 = gather_z(slope_z, whole, 0)
 
-    every_row = remote(sent.at[0:504], got.at[0:504], a_s.at[0], a_r.at[0], there(0, 0))
-    every_row.wait_recv()
+    for g in reversed(FAR_FIRST):
+        few = remote(sent.at[0 : 64 if g else 56], got.at[0 : 64 if g else 56], a_s.at[0], a_r.at[g], there(0, 0))
+        few.wait_recv()
+        rows = pl.ds(pl.multiple_of(lax.rem(z + 8 - g, 8) * 64, 64), 64)
+        Send(got.at[rows], got_l.at[rows], f_s.at[0], f_r.at[0], 1, 0).start()
+        Send(got.at[rows], got_r.at[rows], f_s.at[1], f_r.at[1], -1, 0).start()
     onward = [
         Send(got, got_l, f_s.at[0], f_r.at[0], 1, 0),
         Send(got, got_r, f_s.at[1], f_r.at[1], -1, 0),
     ]
-    for h in onward:
-        h.start()
     late += onward
 
-    def add_loads(ref, block, first, x_local):
+    def add_loads(ref, first, x_local):
         lane = lax.broadcasted_iota(jnp.int32, (64, 128), 1)
         source = lax.broadcasted_iota(jnp.int32, (64, 128), 0)
         key = jnp.zeros((1, 128), F32)
@@ -386,52 +442,59 @@
             loads = jnp.dot(jnp.concatenate([hit, hit], axis=1), values, preferred_element_type=F32)
             at = first + 4 * part
             for c in range(3):
-                total = ff[c, pl.ds(at, 4)] + loads[:, 128 * c : 128 * c + 128].reshape(shape)
-                ff[c, pl.ds(at, 4)] = total
-                aa[c, pl.ds(at, 4)] = ra0[pl.ds(at, 4)] * total
-
-    add_loads(got, 0, 8, 0)
-    add_loads(got, 1, 16, 8)
+                load = loads[:, 128 * c : 128 * c + 128].reshape(shape)
+                ff[c, pl.ds(at, 4)] += load
+                load = ra0[pl.ds(at, 4)] * load
+                aa[c, pl.ds(at, 4)] += load
+                wb[c, pl.ds(at, 4)] += load
+
+    def defect_one(lo, hi):
+        def step(x, count):
+            for c in range(3):
+                at = pl.ds(2 * x, 2 * count)
+                w, n = around(wa, c, 2 * x, 2 * count, 1.0)
+                d = (ff[c, at] - e0[at] * w) + q0[at] * n
+                for i in range(count):
+                    pair = d[2 * i] + d[2 * i + 1]
+                    for j in range(T1):
+                        here = pair[2 * j] + pair[2 * j + 1]
+                        d1[c, x + i, j] = here
+                        a1[c, x + i, j] = ra1[x + i, j] * here
+
+        over(lo, hi, 1, step)
+
+    add_loads(got, 8, 0)
+    add_loads(got, 16, 8)
+    fine_sweep(wb, wa, 10, 22)
+    defect_one(6, 10)
+
+    arrive(mat_len + mat_corners)
+    for lo, hi in ((0, 8), (24, 32)):
+        lax.fori_loop(lo, hi, fine_coefficients, 0)
+        lax.fori_loop(lo // 2, hi // 2, one_coefficients, 0)
+    for lo, hi in ((0, 2), (6, 8)):
+        lax.fori_loop(lo, hi, two_coefficients, 0)
+    arrive(pred_len + pred_corners)
+    for lo, hi in ((0, 8), (24, 32)):
+        lax.fori_loop(lo, hi, start_fine, 0)
+    fine_sweep(wa, wb, 2, 9)
+    fine_sweep(wa, wb, 23, 30)
     onward[0].came()
-    add_loads(got_l, 2, 0, 8)
+    add_loads(got_l, 0, 8)
     onward[1].came()
-    add_loads(got_r, 3, 24, 0)
-
-    def fine_sweep(src, dst, lo, hi):
-        def step(x, _):
-            for c in range(3):
-                w, n = around(src, c, x, 1.0)
-                dst[c, x] = (0.3 * w + aa[c, x]) + b0[x] * n
-            return 0
-
-        lax.fori_loop(lo, hi, step, 0)
-
-    fine_sweep(wa, wb, 1, 31)
-    fine_sweep(wb, wa, 2, 30)
-
-    def defect_one(x, _):
+    add_loads(got_r, 24, 0)
+    fine_sweep(wb, wa, 3, 10)
+    fine_sweep(wb, wa, 22, 29)
+    defect_one(2, 6)
+    defect_one(10, 14)
+
+    def first_correction(x, count):
+        at = pl.ds(x, count)
         for c in range(3):
-            total = None
-            for i in range(2):
-                at = 2 * x + i
-                w, n = around(wa, c, at, 1.0)
-                d = (ff[c, at] - e0[at] * w) + q0[at] * n
-                total = d if total is None else total + d
-            for j in range(T1):
-                here = total[2 * j] + total[2 * j + 1]
-                d1[c, x, j] = here
-                a1[c, x, j] = ra1[x, j] * here
-        return 0
-
-    lax.fori_loop(2, 14, defect_one, 0)
-
-    def first_correction(x, _):
-        for c in range(3):
-            w, n = around(a1, c, x, 4.0)
-            wc[c, x] = 1.3 * w + b1[x] * n
-        return 0
-
-    lax.fori_loop(3, 13, first_correction, 0)
+            w, n = around(a1, c, x, count, 4.0)
+            wc[c, at] = 1.3 * w + b1[at] * n
+
+    over(3, 13, 5, first_correction)
 
     def keep_own(x, _):
         for c in range(3):
@@ -442,14 +505,11 @@
         return 0
 
     for c in range(3):
+        w, n = around(wc, c, 4, 8, 4.0)
+        d = (d1[c, 4:12] - e1[4:12] * w) + q1[4:12] * n
         for x2 in range(4):
-            total = None
-            for i in range(2):
-                x = 4 + 2 * x2 + i
-                w, n = around(wc, c, x, 4.0)
-                d = (d1[c, x] - e1[x] * w) + q1[x] * n
-                total = d if total is None else total + d
-            deft[c, x2] = own_rows_of_pairs(4 * c + x2, [total[j] for j in range(T1)])
+            pair = d[2 * x2] + d[2 * x2 + 1]
+            deft[c, x2] = own_rows_of_pairs(4 * c + x2, [pair[j] for j in range(T1)])
 
     came()
     whole_z = jnp.ones((8, 128), F32)
@@ -604,13 +664,13 @@
     lax.fori_loop(0, X2, correct_one, 0)
 
     def one_sweep(src, dst, lo, hi):
-        def step(x, _):
+        def step(x, count):
+            at = pl.ds(x, count)
             for c in range(3):
-                w, n = around(src, c, x, 4.0)
-                dst[c, x] = (0.3 * w + a1[c, x]) + b1[x] * n
-            return 0
-
-        lax.fori_loop(lo, hi, step, 0)
+                w, n = around(src, c, x, count, 4.0)
+                dst[c, at] = (0.3 * w + a1[c, at]) + b1[at] * n
+
+        over(lo, hi, ONE_GROUP, step)
 
     one_sweep(wc, wd, 1, 15)
     one_sweep(wd, wc, 2, 14)
@@ -628,24 +688,26 @@
     fine_sweep(wb, wa, 5, 27)
     fine_sweep(wa, wb, 6, 26)
 
-    def results(x, _):
+    def results(x, count):
+        at = pl.ds(x, count)
         for c in range(3):
-            w, n = around(wb, c, x, 1.0)
-            value = iq0[x] * w
-            rest = (ff[c, x] - e0[x] * w) + q0[x] * n
-            for j in range(TF):
-                on_v[c, x - 8, pl.ds(j, 8, stride=TF), :] = value[j]
-                on_r[c, x - 8, pl.ds(j, 8, stride=TF), :] = rest[j]
-        return 0
-
-    lax.fori_loop(8, 24, results, 0)
-    outs = [
-        pltpu.make_async_copy(on_v.at[:, :, 8:40, :], out_v, o_s.at[0]),
-        pltpu.make_async_copy(on_r.at[:, :, 8:40, :], out_r, o_s.at[1]),
-    ]
-    for copy in outs:
-        copy.start()
-    every_row.wait_send()
+            w, n = around(wb, c, x, count, 1.0)
+            value = iq0[at] * w
+            rest = (ff[c, at] - e0[at] * w) + q0[at] * n
+            for i in range(count):
+                for j in range(TF):
+                    on_v[c, x - 8 + i, pl.ds(j, 8, stride=TF), :] = value[i, j]
+                    on_r[c, x - 8 + i, pl.ds(j, 8, stride=TF), :] = rest[i, j]
+
+    outs = []
+    for half in range(2):
+        over(8 + 8 * half, 16 + 8 * half, 2, results)
+        rows = slice(8 * half, 8 * half + 8)
+        for k, (src, dst) in enumerate(((on_v, out_v), (on_r, out_r))):
+            copy = pltpu.make_async_copy(src.at[:, rows, 8:40, :], dst.at[:, rows], o_s.at[2 * half + k])
+            copy.start()
+            outs.append(copy)
+    remote(sent.at[0:504], got.at[0:504], a_s.at[0], a_r.at[0], there(0, 0)).wait_send()
     for h in late:
         h.sent()
     for gone in (gone_y0, gone_z0, gone_y1, gone_z1, gone_y2, gone_z2):
@@ -678,15 +740,15 @@
         v(128, 128), *[v(16, 128) for _ in range(4)],
         v(192, 128), *[v(48, 128) for _ in range(4)],
         v(24, 24, 128), v(3, 16, 48, 128), v(3, 16, 48, 128),
-        dma((2,)), dma((16,)), dma((16,)), dma((1,)), dma((1,)), dma((2,)), dma((2,)),
+        dma((2,)), dma((16,)), dma((16,)), dma((1,)), dma((8,)), dma((2,)), dma((2,)),
         dma((3, 8)), dma((3, 8)), dma((3, 8)), dma((3, 8)),
-        dma((7,)), dma((7,)), dma((4,)), dma((4,)), dma((2,)),
+        dma((7,)), dma((7,)), dma((4,)), dma((4,)), dma((4,)),
     ]
     result = jax.ShapeDtypeStruct(predicted.shape, F32)
     return pl.pallas_call(
         body,
         out_shape=(result, result),
-        in_specs=[anywhere, anywhere, smem, smem, vmem, vmem, vmem],
+        in_specs=[pl.BlockSpec(memory_space=pltpu.HBM), pl.BlockSpec(memory_space=pltpu.HBM), smem, smem, vmem, vmem, vmem],
         out_specs=(anywhere, anywhere),
         scratch_shapes=scratch,
         compiler_params=pltpu.CompilerParams(

time: 82.2 us -> 68.1 us (0.83)
  Pallas kernels: 76 us -> 61.4 us
    pallas_call x1, Pallas kernels: 76 us -> 61.4 us  [shards(): pl.pallas_call(body, out_shape=(result, result), in_specs=[pl.BlockSpec(m...]
where the time goes in v1:
time: 68.1 us; the launch traced here: 67.5 us
  Pallas kernels  61.4 us (90%)
  local copies, waits for them, and re-layouts  5.41 us (8%)
    pallas_call x1, Pallas kernels, shards(): pl.pallas_call(body, out_shape=(result, result), in_specs=[pl.BlockSpec(m...  61.4 us
    unnamed x16, local copies, waits for them, and re-layouts  5.41 us

profile of v1, /device:TPU:224, one launch (start us, length us, event | category | flops | bytes accessed | tf_op | source)
XLA Modules:
  0.0 67.5 jit_solution(18168853606682011250)
XLA Ops:
  0.6 0.0 copy-start.6
  0.6 0.0 copy-start.3
  0.7 0.0 copy-start.4
  0.7 0.0 copy-start.5
  0.7 0.6 copy-done.6
  1.3 0.0 copy-done.3
  1.3 0.0 copy-done.4
  1.3 0.0 copy-done.5
  1.3 0.0 copy-start
  1.3 1.1 %copy-done = f32[3,16,32,128]{3,2,1,0:T(8,128)S(1)} copy-done((f32[3,16,32,128]{3,2,1,0:T(8,128)S(1)}, f32[3,16,32,128]{3,2,1,0:T(8,128)}, u32[]{:S(2)}) %copy-start) | copy-done | bytes 786456
  2.5 0.0 copy-start.1
  2.5 0.9 %copy-done.1 = s32[16,32,128]{2,1,0:T(8,128)S(1)} copy-done((s32[16,32,128]{2,1,0:T(8,128)S(1)}, s32[16,32,128]{2,1,0:T(8,128)}, u32[]{:S(2)}) %copy-start.1) | copy-done | bytes 262168
  3.4 0.0 copy-start.2
  3.4 0.9 %copy-done.2 = f32[64,3,128]{2,0,1:T(8,128)S(1)} copy-done((f32[64,3,128]{2,0,1:T(8,128)S(1)}, f32[64,3,128]{2,0,1:T(8,128)}, u32[]{:S(2)}) %copy-start.2) | copy-done | bytes 98328
  4.3 61.4 %shard_map.86 = (f32[3,16,32,128]{3,2,1,0:T(8,128)S(1)}, f32[3,16,32,128]{3,2,1,0:T(8,128)S(1)}) custom-call(f32[3,16,32,128]{3,2,1,0:T(8,128)S(1)} %copy-done, s32[16,32,128]{2,1,0:T(8,128)S(1)} %copy-done.1, f32[8]{0:T(128)S(1)} %copy-done.3, f32[8]{0:T(128)S(1)} %copy-done.4, s32[1,64]{1,0:T(1,128)S(1)} %bitcast.4, s32[1,64]{1,0:T(1,128)S(1)} %bitcast.5, ...), custom_call_target="tpu_custom_call" | custom-call | tf_op jit(solution)/shard_map/pallas_call | solution.py:748
  65.7 0.9 %copy.11 = f32[3,16,32,128]{3,2,1,0:T(8,128)} copy(f32[3,16,32,128]{3,2,1,0:T(8,128)S(1)} %get-tuple-element.4) | data formatting | bytes 1572864
  66.6 0.9 %copy.12 = f32[3,16,32,128]{3,2,1,0:T(8,128)} copy(f32[3,16,32,128]{3,2,1,0:T(8,128)S(1)} %get-tuple-element.5) | data formatting | bytes 1572864
Async XLA Ops:
  0.6 0.7 copy-start.6
  0.6 0.7 copy-start.3
  0.7 0.7 copy-start.4
  0.7 0.7 copy-start.5
  1.3 1.1 %copy-start = (f32[3,16,32,128]{3,2,1,0:T(8,128)S(1)}, f32[3,16,32,128]{3,2,1,0:T(8,128)}, u32[]{:S(2)}) copy-start(f32[3,16,32,128]{3,2,1,0:T(8,128)} %pred_.1) | copy-start | bytes 2359300
  2.5 0.9 %copy-start.1 = (s32[16,32,128]{2,1,0:T(8,128)S(1)}, s32[16,32,128]{2,1,0:T(8,128)}, u32[]{:S(2)}) copy-start(s32[16,32,128]{2,1,0:T(8,128)} %mat.1) | copy-start | bytes 786436
  3.4 0.9 %copy-start.2 = (f32[64,3,128]{2,0,1:T(8,128)S(1)}, f32[64,3,128]{2,0,1:T(8,128)}, u32[]{:S(2)}) copy-start(f32[64,3,128]{2,0,1:T(8,128)} %param.13) | copy-start | bytes 294916
